TPU v7x, 512 devices: a whole 4x4x16 slice. The times are simulated.
512 devices in a mesh: dom: 64 (over x, z), sub: 8 (over y, core).
Axes of the slice: x: 4, y: 4, z: 16, core: 2. Of those that a mesh axis runs over, the one named last changes fastest.
Arguments:
- right_side: float32 [1024, 16, 128], P(('dom', 'sub')), as said below
- diag_blocks: float32 [1024, 128, 128], P(('dom', 'sub')), as said below
- block_values: float32 [1024, 4, 128, 128], P(('dom', 'sub')), as said below
- block_cols: int32 [1024, 4], P(('dom', 'sub')), may hold values from 0 to 31, as said below
- block_count: int32 [1024], P(('dom', 'sub')), may hold values from 0 to 4, as said below
- cell_diagonal: float32 [1024, 128], P(('dom', 'sub')), as said below
Outputs:
- solution_field: float32 [1024, 16, 128], P(('dom', 'sub'))
- residual: float32 [1024, 16, 128], P(('dom', 'sub'))
Inputs may be any that keep to these rules, and one draw needn't show every extreme that they name: `block_cols`: live slots of a block row point to distinct block rows that come after it in the window (positions 0 to 15 are the block rows of the same index of dom, the rest those of the next index); block rows of the last index of dom point only into their own index; dead slots hold 0. `block_count`: the number of live slots, which varies from device to device. `block_values`: entries lie between -1 / 128 and 0. `diag_blocks`: entries lie between -1 / 128 and 0. `cell_diagonal`: every entry exceeds 1 + the live slots of its block row + the live slots of all block rows that couple to its block row, so the operator is strictly diagonally dominant. `right_side`: entries lie between -50 and 50.
All inputs are finite; a program needn't handle non-finite values.
Results may differ from a plain program's by a relative error of at most 0.00065.
Values sent between devices are 32-bit elements; how exact they have to be, the bound alone decides.
A program may use at most 64 MiB of HBM per device.

v0:
```python
import jax
import jax.numpy as jnp
from jax import lax
from jax.sharding import PartitionSpec as P

K = 4
ITERS = 3
PRECISE = lax.Precision.HIGHEST


def passed_along(x, axis, by):
    peers = lax.axis_size(axis)
    pairs = [(i, i + by) for i in range(peers) if 0 <= i + by < peers]
    return lax.ppermute(x, axis, pairs)


def local(right_side, diag_blocks, block_values, block_cols, block_count, cell_diagonal):
    rows_dev = right_side.shape[0]
    group_rows = lax.axis_size("sub") * rows_dev
    upper_part = jnp.triu(diag_blocks, 1)
    live_slots = jnp.arange(K, dtype=jnp.int32)[None, :] < block_count[:, None]
    window_ids = jnp.arange(2 * group_rows, dtype=jnp.int32)
    picker = (
        (block_cols[:, :, None] == window_ids[None, None, :]) & live_slots[:, :, None]
    ).astype(jnp.float32)

    def local_dots(first, second):
        return jnp.sum(first * second, axis=(0, 2))

    def residual_sum(residual_now, precond_now):
        return lax.psum(local_dots(residual_now, precond_now), ("dom", "sub"))

    solution_field = jnp.zeros_like(right_side)
    residual = right_side
    precond_res = residual / cell_diagonal[:, None, :]
    direction = precond_res
    precond_dot = residual_sum(residual, precond_res)
    for iteration in range(ITERS):
        own_part = jnp.einsum("rab,rzb->rza", upper_part, direction, precision=PRECISE)
        own_part = own_part + jnp.einsum("rba,rzb->rza", upper_part, direction, precision=PRECISE)
        own_part = own_part + cell_diagonal[:, None, :] * direction
        own_group = lax.all_gather(direction, "sub", axis=0, tiled=True)
        next_group = passed_along(own_group, "dom", -1)
        window = jnp.concatenate([own_group, next_group], axis=0)
        far_rows = jnp.einsum("rkw,wzb->rkzb", picker, window, precision=PRECISE)
        forward = jnp.einsum("rkab,rkzb->rza", block_values, far_rows, precision=PRECISE)
        back_terms = jnp.einsum("rkba,rzb->rkza", block_values, direction, precision=PRECISE)
        spread = jnp.einsum("rkw,rkza->wza", picker, back_terms, precision=PRECISE)
        incoming = passed_along(spread[group_rows:], "dom", 1)
        back_own = lax.psum_scatter(
            spread[:group_rows] + incoming, "sub", scatter_dimension=0, tiled=True
        )
        image_vec = own_part + forward + back_own
        curvature = lax.psum(local_dots(direction, image_vec), ("dom", "sub"))
        step_size = precond_dot / curvature
        solution_field = solution_field + step_size[None, :, None] * direction
        residual = residual - step_size[None, :, None] * image_vec
        if iteration + 1 < ITERS:
            precond_res = residual / cell_diagonal[:, None, :]
            new_dot = residual_sum(residual, precond_res)
            direction = precond_res + (new_dot / precond_dot)[None, :, None] * direction
            precond_dot = new_dot
    return (solution_field, residual)


def solution(mesh):
    return jax.shard_map(
        local,
        mesh=mesh,
        in_specs=(
            P(("dom", "sub"), None, None),
            P(("dom", "sub"), None, None),
            P(("dom", "sub"), None, None, None),
            P(("dom", "sub"), None),
            P(("dom", "sub")),
            P(("dom", "sub"), None),
        ),
        out_specs=(P(("dom", "sub"), None, None), P(("dom", "sub"), None, None)),
        check_vma=False,
    )
```

profile of v0, /device:TPU:1, one launch (start us, length us, event | category | flops | bytes accessed | tf_op | source)
XLA Modules:
  0.0 715.4 jit_solution(11586665640421009732)
XLA Ops:
  7.2 0.8 broadcast_divide_fusion
  8.0 19.6 %all_gather.9 = f32[16,16,128]{2,1,0:T(8,128)S(1)} all-gather(f32[2,16,128]{2,1,0:T(8,128)S(1)} %broadcast_divide_fusion), channel_id=1, replica_groups=mesh['dom'=64,'sub'=8] {'sub'}, dimensions={0}, use_global_device_ids=true | all-gather | bytes 147456 | tf_op jit(solution)/shard_map/all_gather | solution.py:42
  27.6 1.4 collective-permute-start
  30.3 4.0 collective-permute-start.1
  35.0 1.7 collective-permute-done.1
  36.7 0.7 copy_add_fusion.2
  37.5 0.5 convolution_bitcast_fusion.5
  38.2 37.2 %reduce-scatter.4.cloned.1.call-done = f32[2,16,128]{2,1,0:T(8,128)} async-done(((f32[16,16,128]{2,1,0:T(8,128)}), f32[2,16,128]{2,1,0:T(8,128)}) %reduce-scatter.4.cloned.1.call-update) | async-done | bytes 16400 | tf_op jit(solution)/shard_map/reduce_scatter | solution.py:50
  75.4 0.8 multiply_reduce_fusion.4
  76.2 105.7 %all-reduce = (f32[16]{0:T(128)S(1)}, f32[16]{0:T(128)S(1)}) all-reduce(f32[16]{0:T(128)S(1)} %get-tuple-element.3, f32[16]{0:T(128)S(1)} %get-tuple-element.2), channel_id=1, replica_groups=mesh['dom'=64,'sub'=8] {'dom','sub'}, use_global_device_ids=true, to_apply=%region_1.2 | all-reduce | flops 32 | bytes 256 | tf_op jit(solution)/shard_map/psum | solution.py:31
  182.2 99.4 %psum.44 = f32[16]{0:T(128)S(1)} all-reduce(f32[16]{0:T(128)S(1)} %get-tuple-element.12), channel_id=1, replica_groups=mesh['dom'=64,'sub'=8] {'dom','sub'}, use_global_device_ids=true, to_apply=%region_6.7 | all-reduce | flops 16 | bytes 128 | tf_op jit(solution)/shard_map/psum | solution.py:31
  281.7 13.2 %all_gather.10 = f32[16,16,128]{2,1,0:T(8,128)S(1)} all-gather(f32[2,16,128]{2,1,0:T(8,128)S(1)} %multiply_add_fusion.2), channel_id=1, replica_groups=mesh['dom'=64,'sub'=8] {'sub'}, dimensions={0}, use_global_device_ids=true | all-gather | bytes 147456 | tf_op jit(solution)/shard_map/all_gather | solution.py:42
  295.3 1.3 collective-permute-start.2
  297.1 4.0 collective-permute-start.3
  301.3 0.7 collective-permute-done.2
  302.4 1.0 collective-permute-done.3
  303.4 0.7 copy_add_fusion.1
  304.2 0.5 convolution_bitcast_fusion.4
  305.0 33.6 %reduce-scatter.6.cloned.1.call-done = f32[2,16,128]{2,1,0:T(8,128)} async-done(((f32[16,16,128]{2,1,0:T(8,128)}), f32[2,16,128]{2,1,0:T(8,128)}) %reduce-scatter.6.cloned.1.call-update) | async-done | bytes 16400 | tf_op jit(solution)/shard_map/reduce_scatter | solution.py:50
  338.5 0.8 multiply_reduce_fusion.2
  339.4 105.7 %psum.45 = f32[16]{0:T(128)S(1)} all-reduce(f32[16]{0:T(128)S(1)} %get-tuple-element.10), channel_id=1, replica_groups=mesh['dom'=64,'sub'=8] {'dom','sub'}, use_global_device_ids=true, to_apply=%region_9.10 | all-reduce | flops 16 | bytes 128 | tf_op jit(solution)/shard_map/psum | solution.py:54
  445.3 99.2 %psum.46 = f32[16]{0:T(128)S(1)} all-reduce(f32[16]{0:T(128)S(1)} %get-tuple-element.8), channel_id=1, replica_groups=mesh['dom'=64,'sub'=8] {'dom','sub'}, use_global_device_ids=true, to_apply=%region_11.12 | all-reduce | flops 16 | bytes 128 | tf_op jit(solution)/shard_map/psum | solution.py:31
  544.6 13.2 %all_gather.11 = f32[16,16,128]{2,1,0:T(8,128)S(1)} all-gather(f32[2,16,128]{2,1,0:T(8,128)S(1)} %multiply_add_fusion.1), channel_id=1, replica_groups=mesh['dom'=64,'sub'=8] {'sub'}, dimensions={0}, use_global_device_ids=true | all-gather | bytes 147456 | tf_op jit(solution)/shard_map/all_gather | solution.py:42
  558.2 1.3 collective-permute-start.4
  560.0 4.0 collective-permute-start.5
  564.2 0.7 collective-permute-done.4
  565.3 1.0 collective-permute-done.5
  566.3 0.7 copy_add_fusion
  567.8 33.7 %reduce-scatter.8.cloned.1.call-done = f32[2,16,128]{2,1,0:T(8,128)} async-done(((f32[16,16,128]{2,1,0:T(8,128)}), f32[2,16,128]{2,1,0:T(8,128)}) %reduce-scatter.8.cloned.1.call-update) | async-done | bytes 16400 | tf_op jit(solution)/shard_map/reduce_scatter | solution.py:50
  601.5 0.8 multiply_reduce_fusion
  602.4 105.8 %psum.47 = f32[16]{0:T(128)S(1)} all-reduce(f32[16]{0:T(128)S(1)} %get-tuple-element.6), channel_id=1, replica_groups=mesh['dom'=64,'sub'=8] {'dom','sub'}, use_global_device_ids=true, to_apply=%region_14.15 | all-reduce | flops 16 | bytes 128 | tf_op jit(solution)/shard_map/psum | solution.py:54
  708.2 0.7 multiply_subtract_fusion
  (55 shorter events, 6.7 us)
Async XLA Ops:
  7.2 21.9 %copy-start = (f32[2,4,128,128]{3,2,1,0:T(8,128)S(1)}, f32[2,4,128,128]{3,2,1,0:T(8,128)}, u32[]{:S(2)}) copy-start(f32[2,4,128,128]{3,2,1,0:T(8,128)} %param.8) | copy-start | bytes 1572868
  7.2 68.2 %reduce-scatter.4.cloned.1.call-start = ((), (), s32[]{:S(2)}) async-start(), calls=%async_computation.3 | async-start | bytes 147456 | tf_op jit(solution)/shard_map/reduce_scatter | solution.py:50
  8.0 21.0 %copy-start.5 = (s32[2]{0:T(128)S(1)}, s32[2]{0:T(128)}, u32[]{:S(2)}) copy-start(s32[2]{0:T(128)} %param.10) | copy-start | bytes 28
  8.0 21.1 %copy-start.2 = (f32[2,16,128]{2,1,0:T(8,128)S(1)}, f32[2,16,128]{2,1,0:T(8,128)}, u32[]{:S(2)}) copy-start(f32[2,16,128]{2,1,0:T(8,128)} %param.6) | copy-start | bytes 49156
  27.6 1.5 copy-start.3
  27.6 7.0 collective-permute-start
  29.1 0.7 copy-start.4
  30.2 4.1 copy-start.1
  30.3 6.4 collective-permute-start.1
  37.4 301.1 %reduce-scatter.6.cloned.1.call-start = ((), (), s32[]{:S(2)}) async-start(), calls=%async_computation.4 | async-start | bytes 147456 | tf_op jit(solution)/shard_map/reduce_scatter | solution.py:50
  295.3 6.8 collective-permute-start.2
  297.1 6.4 collective-permute-start.3
  304.2 297.4 %reduce-scatter.8.cloned.1.call-start = ((), (), s32[]{:S(2)}) async-start(), calls=%async_computation.5 | async-start | bytes 147456 | tf_op jit(solution)/shard_map/reduce_scatter | solution.py:50
  558.2 6.8 collective-permute-start.4
  560.0 6.4 collective-permute-start.5
Sparse Core Ops, SparseCore 0:
  37.5 37.8 reduce-scatter.3
  304.3 34.2 reduce-scatter.5
  567.2 34.3 reduce-scatter.7
where the time goes:
time: 717 us; the launch traced here: 715 us
  blocking collectives  562 us (78%)
  waiting for transfers between devices  110 us (15%)
  starting transfers between devices  16.1 us (2%)
  between operations  14 us (2%)
    psum x3, blocking collectives, residual_sum(): return lax.psum(local_dots(residual_now, precond_now), ('dom', 'sub'))  304 us
    psum x2, blocking collectives, local(): curvature = lax.psum(local_dots(direction, image_vec), ('dom', 'sub'))  212 us
    reduce_scatter x3, waiting for transfers between devices, local(): lax.psum_scatter(spread[:group_rows] + incoming, 'sub', scatter_dimension...  104 us
    all_gather x3, blocking collectives, local(): own_group = lax.all_gather(direction, 'sub', axis=0, tiled=True)  46.1 us
    ppermute x6, starting transfers between devices, passed_along(): return lax.ppermute(x, axis, pairs)  16 us
  transfers between devices with their start and end apart: 9, of which 8 were waited for; matrix products, arithmetic and copies ran while one was open for 1% of the time, Pallas kernels for 0%

commit v1 on v0

--- a/solution.py
+++ b/solution.py
@@ -39,7 +39,12 @@
         own_part = jnp.einsum("rab,rzb->rza", upper_part, direction, precision=PRECISE)
         own_part = own_part + jnp.einsum("rba,rzb->rza", upper_part, direction, precision=PRECISE)
         own_part = own_part + cell_diagonal[:, None, :] * direction
-        own_group = lax.all_gather(direction, "sub", axis=0, tiled=True)
+        own_group = jnp.concatenate(
+            lax.all_to_all(
+                jnp.stack([direction for _ in range(lax.axis_size("sub"))]), "sub", 0, 0
+            ),
+            0,
+        )
         next_group = passed_along(own_group, "dom", -1)
         window = jnp.concatenate([own_group, next_group], axis=0)
         far_rows = jnp.einsum("rkw,wzb->rkzb", picker, window, precision=PRECISE)

time: 717 us -> 689 us (0.961)
  blocking collectives: 562 us -> 516 us
  starting transfers between devices: 16.1 us -> 28.7 us
    all_gather x3 -> x0, blocking collectives: 46.1 us -> none  [local(): own_group = lax.all_gather(direction, 'sub', axis=0, tiled=True)]
    all_to_all x0 -> x3, starting transfers between devices: none -> 18.2 us  [local(): lax.all_to_all(jnp.stack([direction for _ in range(lax.axis_size('sub'))]...]
    reduce_scatter x3, waiting for transfers between devices: 104 us -> 94.9 us  [local(): lax.psum_scatter(spread[:group_rows] + incoming, 'sub', scatter_dimension...]
  transfers between devices with their start and end apart: 9 -> 12, of which waited for: 8 -> 9; matrix products, arithmetic and copies ran while one was open for 1% -> 1% of each run, Pallas kernels for 0% -> 0%
where the time goes in v1:
time: 689 us; the launch traced here: 687 us
  blocking collectives  516 us (75%)
  waiting for transfers between devices  112 us (16%)
  starting transfers between devices  28.7 us (4%)
  between operations  14 us (2%)
    psum x3, blocking collectives, residual_sum(): return lax.psum(local_dots(residual_now, precond_now), ('dom', 'sub'))  305 us
    psum x2, blocking collectives, local(): curvature = lax.psum(local_dots(direction, image_vec), ('dom', 'sub'))  211 us
    reduce_scatter x3, waiting for transfers between devices, local(): lax.psum_scatter(spread[:group_rows] + incoming, 'sub', scatter_dimension...  94.9 us
    all_to_all x3, starting transfers between devices, local(): lax.all_to_all(jnp.stack([direction for _ in range(lax.axis_size('sub'))]...  18.2 us
  transfers between devices with their start and end apart: 12, of which 9 were waited for; matrix products, arithmetic and copies ran while one was open for 1% of the time, Pallas kernels for 0%

profile of v1, /device:TPU:1, one launch (start us, length us, event | category | flops | bytes accessed | tf_op | source)
XLA Modules:
  0.0 687.1 jit_solution(12412002943891612536)
XLA Ops:
  7.2 0.8 broadcast_divide_fusion
  8.0 0.7 stack.6
  8.6 10.3 %all-to-all-start = ((f32[8,2,16,128]{3,2,1,0:T(8,128)}), f32[8,2,16,128]{3,2,1,0:T(8,128)S(1)}, u32[]{:S(2)}, u32[]{:S(2)}) async-start(f32[8,2,16,128]{3,2,1,0:T(8,128)} %stack.6), calls=%async_computation | async-start | bytes 262144 | tf_op jit(solution)/shard_map/all_to_all | solution.py:43
  20.8 1.3 collective-permute-start.1
  22.4 1.8 all-to-all-done
  24.2 1.3 collective-permute-start
  25.5 0.7 copy_add_fusion.2
  26.2 4.0 collective-permute-done
  31.3 35.4 %reduce-scatter.4.cloned.1.call-done = f32[2,16,128]{2,1,0:T(8,128)} async-done(((f32[16,16,128]{2,1,0:T(8,128)}), f32[2,16,128]{2,1,0:T(8,128)}) %reduce-scatter.4.cloned.1.call-update) | async-done | bytes 16400 | tf_op jit(solution)/shard_map/reduce_scatter | solution.py:55
  66.7 0.8 multiply_reduce_fusion.4
  67.5 105.8 %all-reduce = (f32[16]{0:T(128)S(1)}, f32[16]{0:T(128)S(1)}) all-reduce(f32[16]{0:T(128)S(1)} %get-tuple-element.3, f32[16]{0:T(128)S(1)} %get-tuple-element.2), channel_id=1, replica_groups=mesh['dom'=64,'sub'=8] {'dom','sub'}, use_global_device_ids=true, to_apply=%region_1.2 | all-reduce | flops 32 | bytes 256 | tf_op jit(solution)/shard_map/psum | solution.py:31
  173.4 99.4 %psum.44 = f32[16]{0:T(128)S(1)} all-reduce(f32[16]{0:T(128)S(1)} %get-tuple-element.12), channel_id=1, replica_groups=mesh['dom'=64,'sub'=8] {'dom','sub'}, use_global_device_ids=true, to_apply=%region_6.7 | all-reduce | flops 16 | bytes 128 | tf_op jit(solution)/shard_map/psum | solution.py:31
  273.9 3.9 all-to-all-start.1
  278.4 2.7 collective-permute-start.3
  281.4 1.8 all-to-all-done.1
  283.2 1.3 collective-permute-start.2
  284.5 0.7 copy_add_fusion.1
  285.2 4.0 collective-permute-done.2
  290.3 29.8 %reduce-scatter.6.cloned.1.call-done = f32[2,16,128]{2,1,0:T(8,128)} async-done(((f32[16,16,128]{2,1,0:T(8,128)}), f32[2,16,128]{2,1,0:T(8,128)}) %reduce-scatter.6.cloned.1.call-update) | async-done | bytes 16400 | tf_op jit(solution)/shard_map/reduce_scatter | solution.py:55
  320.0 0.8 multiply_reduce_fusion.2
  320.9 105.7 %psum.45 = f32[16]{0:T(128)S(1)} all-reduce(f32[16]{0:T(128)S(1)} %get-tuple-element.10), channel_id=1, replica_groups=mesh['dom'=64,'sub'=8] {'dom','sub'}, use_global_device_ids=true, to_apply=%region_9.10 | all-reduce | flops 16 | bytes 128 | tf_op jit(solution)/shard_map/psum | solution.py:59
  426.8 99.4 %psum.46 = f32[16]{0:T(128)S(1)} all-reduce(f32[16]{0:T(128)S(1)} %get-tuple-element.8), channel_id=1, replica_groups=mesh['dom'=64,'sub'=8] {'dom','sub'}, use_global_device_ids=true, to_apply=%region_11.12 | all-reduce | flops 16 | bytes 128 | tf_op jit(solution)/shard_map/psum | solution.py:31
  527.3 3.9 all-to-all-start.2
  531.7 2.7 collective-permute-start.5
  534.7 1.8 all-to-all-done.2
  536.5 1.3 collective-permute-start.4
  537.8 0.7 copy_add_fusion
  538.5 4.0 collective-permute-done.4
  543.6 29.8 %reduce-scatter.8.cloned.1.call-done = f32[2,16,128]{2,1,0:T(8,128)} async-done(((f32[16,16,128]{2,1,0:T(8,128)}), f32[2,16,128]{2,1,0:T(8,128)}) %reduce-scatter.8.cloned.1.call-update) | async-done | bytes 16400 | tf_op jit(solution)/shard_map/reduce_scatter | solution.py:55
  573.4 0.8 multiply_reduce_fusion
  574.2 105.7 %psum.47 = f32[16]{0:T(128)S(1)} all-reduce(f32[16]{0:T(128)S(1)} %get-tuple-element.6), channel_id=1, replica_groups=mesh['dom'=64,'sub'=8] {'dom','sub'}, use_global_device_ids=true, to_apply=%region_14.15 | all-reduce | flops 16 | bytes 128 | tf_op jit(solution)/shard_map/psum | solution.py:59
  679.9 0.7 multiply_subtract_fusion
  (61 shorter events, 9.5 us)
Async XLA Ops:
  7.2 11.8 %copy-start = (f32[2,4,128,128]{3,2,1,0:T(8,128)S(1)}, f32[2,4,128,128]{3,2,1,0:T(8,128)}, u32[]{:S(2)}) copy-start(f32[2,4,128,128]{3,2,1,0:T(8,128)} %param.8) | copy-start | bytes 1572868
  8.6 10.3 %copy-start.5 = (s32[2]{0:T(128)S(1)}, s32[2]{0:T(128)}, u32[]{:S(2)}) copy-start(s32[2]{0:T(128)} %param.10) | copy-start | bytes 28
  8.6 10.4 %copy-start.2 = (f32[2,16,128]{2,1,0:T(8,128)S(1)}, f32[2,16,128]{2,1,0:T(8,128)}, u32[]{:S(2)}) copy-start(f32[2,16,128]{2,1,0:T(8,128)} %param.6) | copy-start | bytes 49156
  8.6 15.6 %all-to-all-start = ((f32[8,2,16,128]{3,2,1,0:T(8,128)}), f32[8,2,16,128]{3,2,1,0:T(8,128)S(1)}, u32[]{:S(2)}, u32[]{:S(2)}) async-start(f32[8,2,16,128]{3,2,1,0:T(8,128)} %stack.6), calls=%async_computation | async-start | bytes 262144 | tf_op jit(solution)/shard_map/all_to_all | solution.py:43
  18.9 0.7 copy-start.3
  18.9 47.8 %reduce-scatter.4.cloned.1.call-start = ((), (), s32[]{:S(2)}) async-start(), calls=%async_computation.6 | async-start | bytes 147456 | tf_op jit(solution)/shard_map/reduce_scatter | solution.py:55
  19.6 0.7 copy-start.4
  20.7 1.4 copy-start.1
  20.8 4.7 collective-permute-start.1
  24.2 6.0 collective-permute-start
  273.9 9.2 %all-to-all-start.1 = ((f32[8,2,16,128]{3,2,1,0:T(8,128)}), f32[8,2,16,128]{3,2,1,0:T(8,128)S(1)}, u32[]{:S(2)}, u32[]{:S(2)}) async-start(f32[8,2,16,128]{3,2,1,0:T(8,128)} %stack.7), calls=%async_computation.2 | async-start | bytes 262144 | tf_op jit(solution)/shard_map/all_to_all | solution.py:43
  277.9 42.1 %reduce-scatter.6.cloned.1.call-start = ((), (), s32[]{:S(2)}) async-start(), calls=%async_computation.7 | async-start | bytes 147456 | tf_op jit(solution)/shard_map/reduce_scatter | solution.py:55
  278.4 6.1 collective-permute-start.3
  283.2 6.0 collective-permute-start.2
  527.3 9.2 %all-to-all-start.2 = ((f32[8,2,16,128]{3,2,1,0:T(8,128)}), f32[8,2,16,128]{3,2,1,0:T(8,128)S(1)}, u32[]{:S(2)}, u32[]{:S(2)}) async-start(f32[8,2,16,128]{3,2,1,0:T(8,128)} %stack.8), calls=%async_computation.4 | async-start | bytes 262144 | tf_op jit(solution)/shard_map/all_to_all | solution.py:43
  531.2 42.2 %reduce-scatter.8.cloned.1.call-start = ((), (), s32[]{:S(2)}) async-start(), calls=%async_computation.8 | async-start | bytes 147456 | tf_op jit(solution)/shard_map/reduce_scatter | solution.py:55
  531.7 6.1 collective-permute-start.5
  536.5 6.0 collective-permute-start.4
Sparse Core Ops, SparseCore 0:
  26.3 40.2 reduce-scatter.3
  285.3 34.6 reduce-scatter.5
  538.6 34.6 reduce-scatter.7
